TPU v7x, 32 devices: a whole 2x2x4 slice. The times are simulated.
32 devices in a mesh: groups: 2 (over y), ep: 4 (over z), tp: 4 (over x, core).
Axes of the slice: x: 2, y: 2, z: 4, core: 2. Of those that a mesh axis runs over, the one named last changes fastest.
Arguments:
- x_rows: bfloat16 [128, 4096], P(('groups', 'ep', 'tp')), parts along dimension 0, may hold values from -6 to 6
- queries: bfloat16 [128, 4096], P(('groups', 'ep', 'tp')), parts along dimension 0, may hold values from -80 to 80
- key_cache: bfloat16 [128, 64, 256], P(('groups', 'ep', 'tp')), parts along dimension 0, may hold values from -4 to 4
- value_cache: bfloat16 [128, 64, 256], P(('groups', 'ep', 'tp')), parts along dimension 0, may hold values from -6 to 6
- new_key: bfloat16 [128, 256], P(('groups', 'ep', 'tp')), parts along dimension 0, may hold values from -4 to 4
- new_value: bfloat16 [128, 256], P(('groups', 'ep', 'tp')), parts along dimension 0, may hold values from -6 to 6
- lengths: int32 [128], P(('groups', 'ep', 'tp')), parts along dimension 0, may hold values from 2 to 64, as said below
- norm_gain: bfloat16 [4096], replicated, may hold values from 0.099609375 to 1.8984375
- expert_ids: int32 [128, 8], P(('groups', 'ep', 'tp')), parts along dimension 0, may hold values from 0 to 15, all different within a row; in each aligned block of 4 rows (0 to 3, 4 to 7, ...) at most 4 rows name the same one
- gate_probs: float32 [128, 8], P(('groups', 'ep', 'tp')), parts along dimension 0, may hold values from 0.02 to 0.4
- expert_place: int32 [16], replicated, may hold values from 0 to 15, each once
- w_gate: bfloat16 [16, 4096, 1536], P('ep', None, 'tp'), may hold values from -0.09375 to 0.09375
- w_up: bfloat16 [16, 4096, 1536], P('ep', None, 'tp'), may hold values from -0.09375 to 0.09375
- w_down: bfloat16 [16, 1536, 4096], P('ep', 'tp'), may hold values from -0.15625 to 0.15625
Outputs:
- layer_out: bfloat16 [128, 4096], P(('groups', 'ep', 'tp')), parts along dimension 0
- expert_mix: bfloat16 [128, 4096], P(('groups', 'ep', 'tp')), parts along dimension 0
There are 2 independent parts, one for each index of `groups`. A program takes and returns all parts, laid end to end along the dimension named above; an argument that names none is the same for every part. Nothing has to cross between parts.
Inputs may be any that keep to these rules, and one draw needn't show every extreme that they name: `expert_ids`: each row names 8 different experts; among the 4 rows of one device no expert is named more than 4 times. `expert_place`: a permutation; slot j lies on index j // 4 of ep. `lengths`: some request has exactly 64 positions.
All inputs are finite; a program needn't handle non-finite values.
Results may differ from a plain program's by a relative error of at most 0.012.
Values may be sent and summed in bfloat16 or wider, within the bound.
A program may use at most 128 MiB of HBM per device.

v0:
```python
import jax
import jax.numpy as jnp
from jax import lax
from jax.sharding import PartitionSpec as P

HEAD_DIM = 128
Q_HEADS = 32
KV_HEADS = 2


highest = lax.Precision.HIGHEST


def attend(queries, key_cache, value_cache, new_key, new_value, lengths):
    row_count = queries.shape[0]
    span = key_cache.shape[1]
    groups = Q_HEADS // KV_HEADS
    factor = HEAD_DIM ** (-0.5)
    query = queries.astype(jnp.float32).reshape(row_count, KV_HEADS, groups, HEAD_DIM)
    cached_keys = key_cache.astype(jnp.float32).reshape(row_count, span, KV_HEADS, HEAD_DIM)
    cached_values = value_cache.astype(jnp.float32).reshape(row_count, span, KV_HEADS, HEAD_DIM)
    fresh_key = new_key.astype(jnp.float32).reshape(row_count, KV_HEADS, HEAD_DIM)
    fresh_value = new_value.astype(jnp.float32).reshape(row_count, KV_HEADS, HEAD_DIM)
    scores = jnp.einsum("rgjd,rpgd->rgjp", query, cached_keys, precision=highest) * factor
    own_score = jnp.einsum("rgjd,rgd->rgj", query, fresh_key, precision=highest) * factor
    valid = (jnp.arange(span, dtype=jnp.int32)[None, :] < lengths[:, None])[:, None, None, :]
    masked = jnp.where(valid, scores, -1e30)
    peak_all = jnp.maximum(jnp.max(masked, axis=3), own_score)
    weights = jnp.where(valid, jnp.exp(masked - peak_all[..., None]), 0.0)
    own_weight = jnp.exp(own_score - peak_all)
    denominator = jnp.sum(weights, axis=3) + own_weight
    summed = jnp.einsum("rgjp,rpgd->rgjd", weights, cached_values, precision=highest)
    summed = summed + own_weight[..., None] * fresh_value[:, :, None, :]
    return (summed / denominator[..., None]).reshape(row_count, Q_HEADS * HEAD_DIM)


def local(
    x_rows,
    queries,
    key_cache,
    value_cache,
    new_key,
    new_value,
    lengths,
    norm_gain,
    expert_ids,
    gate_probs,
    expert_place,
    w_gate,
    w_up,
    w_down,
):
    tp_count = lax.axis_size("tp")
    ep_count = lax.axis_size("ep")
    row_count = x_rows.shape[0]
    width = x_rows.shape[1]
    stream = x_rows.astype(jnp.float32) + attend(
        queries, key_cache, value_cache, new_key, new_value, lengths
    )
    scaled = lax.rsqrt(jnp.mean(stream * stream, axis=1, keepdims=True) + 1e-06)
    normed = (stream * scaled * norm_gain.astype(jnp.float32)).astype(jnp.bfloat16)
    experts_total = expert_place.shape[0]
    local_experts = w_gate.shape[0]
    top_count = expert_ids.shape[1]
    capacity = max(2, 2 * row_count * top_count // experts_total)
    expert_range = jnp.arange(experts_total, dtype=jnp.int32)
    target = jnp.sum(
        jnp.where(expert_ids[:, :, None] == expert_range, expert_place, 0), axis=2
    ).reshape(-1)
    hits = (target[:, None] == expert_range[None, :]).astype(jnp.int32)
    earlier = jnp.sum((jnp.cumsum(hits, axis=0) - hits) * hits, axis=1)
    slot_index = target * capacity + earlier
    slot_range = jnp.arange(experts_total * capacity, dtype=jnp.int32)
    spread = jnp.any(
        slot_index.reshape(row_count, top_count)[:, :, None] == slot_range, axis=1
    ).astype(jnp.bfloat16)
    group_rows, group_spread = (
        lax.all_gather(normed, "tp", axis=0, tiled=True),
        lax.all_gather(spread, "tp", axis=0, tiled=True),
    )
    layout = group_spread.reshape(tp_count, row_count, experts_total, capacity)
    placed_rows = jnp.einsum(
        "trjc,trd->jtcd",
        layout,
        group_rows.reshape(tp_count, row_count, width),
        preferred_element_type=jnp.float32,
    ).astype(jnp.bfloat16)
    arrived = lax.all_to_all(
        placed_rows.reshape(ep_count, local_experts, tp_count * capacity, width),
        "ep",
        split_axis=0,
        concat_axis=2,
        tiled=True,
    )
    gate_act = jnp.einsum("aesd,edf->aesf", arrived, w_gate, preferred_element_type=jnp.float32)
    up_act = jnp.einsum("aesd,edf->aesf", arrived, w_up, preferred_element_type=jnp.float32)
    partial_value = jnp.einsum(
        "aesf,efd->aesd",
        (jax.nn.silu(gate_act) * up_act).astype(jnp.bfloat16),
        w_down,
        preferred_element_type=jnp.float32,
    ).astype(jnp.bfloat16)
    returned = lax.all_to_all(partial_value, "ep", split_axis=2, concat_axis=0, tiled=True)
    terms = returned.astype(jnp.float32).reshape(ep_count, local_experts, tp_count, capacity, width)
    own_slots = lax.psum_scatter(
        terms.astype(jnp.bfloat16), "tp", scatter_dimension=2, tiled=True
    ).astype(jnp.float32)
    own_slots = own_slots.reshape(experts_total * capacity, width)
    chosen = own_slots[slot_index].reshape(row_count, top_count, width)
    mixed = jnp.sum(chosen * gate_probs[:, :, None], axis=1)
    return ((stream + mixed).astype(jnp.bfloat16), mixed.astype(jnp.bfloat16))


def solution(mesh):
    return jax.shard_map(
        local,
        mesh=mesh,
        in_specs=(
            P(("groups", "ep", "tp"), None),
            P(("groups", "ep", "tp"), None),
            P(("groups", "ep", "tp"), None, None),
            P(("groups", "ep", "tp"), None, None),
            P(("groups", "ep", "tp"), None),
            P(("groups", "ep", "tp"), None),
            P(("groups", "ep", "tp")),
            P(),
            P(("groups", "ep", "tp"), None),
            P(("groups", "ep", "tp"), None),
            P(),
            P("ep", None, "tp"),
            P("ep", None, "tp"),
            P("ep", "tp", None),
        ),
        out_specs=(P(("groups", "ep", "tp"), None), P(("groups", "ep", "tp"), None)),
        check_vma=False,
    )
```

profile of v0, /device:TPU:0, one launch (start us, length us, event | category | flops | bytes accessed | tf_op | source)
XLA Modules:
  0.0 222.3 jit_solution(1020213614959721247)
XLA Ops:
  7.2 0.8 iota_compare_fusion.3
  8.0 0.8 copy.50
  8.7 0.7 reshape.156
  9.6 1.2 fusion.25
  10.8 0.2 fusion.13
  11.0 0.7 reshape.135
  11.7 0.3 fusion.5
  12.0 0.9 multiply_reduce_fusion
  12.9 0.7 convert_element_type.52
  13.6 0.8 fusion.14
  14.4 6.5 %all-gather = bf16[4,4,4096]{2,1,0:T(4,128)(2,1)S(1)} all-gather(bf16[1,4,4096]{2,1,0:T(4,128)(2,1)S(1)} %fusion.14), channel_id=1, replica_groups=mesh['groups'=2,'ep'=4,'tp'=4] {'tp'}, dimensions={0}, use_global_device_ids=true | all-gather | bytes 163840 | tf_op jit(solution)/shard_map/all_gather | solution.py:78
  20.9 0.9 select_reduce_fusion.1
  22.0 0.2 select_reduce_fusion
  22.4 5.2 %all-gather.1 = bf16[4,4,64]{2,1,0:T(4,128)(2,1)S(1)} all-gather(bf16[1,4,64]{2,1,0:T(4,128)(2,1)S(1)} %convert_bitcast_fusion), channel_id=1, replica_groups=mesh['groups'=2,'ep'=4,'tp'=4] {'tp'}, dimensions={0}, use_global_device_ids=true | all-gather | bytes 2560 | tf_op jit(solution)/shard_map/all_gather | solution.py:79
  28.0 0.8 fusion
  28.7 2.2 %reshape.129 = bf16[4,4,16,4096]{3,1,0,2:T(4,128)(2,1)} reshape(bf16[16,4,4,4096]{3,0,2,1:T(8,128)(2,1)S(1)} %fusion) | data formatting | bytes 4194304 | tf_op jit(solution)/shard_map/reshape | solution.py:89
  31.0 2.6 %copy.41 = bf16[4,4,16,4096]{3,1,2,0:T(4,128)(2,1)S(1)} copy(bf16[4,4,16,4096]{3,1,0,2:T(4,128)(2,1)} %reshape.129) | data formatting | bytes 4194304 | tf_op jit(solution)/shard_map/reshape | solution.py:89
  33.6 53.8 %all_to_all.33 = bf16[4,4,16,4096]{3,1,2,0:T(4,128)(2,1)S(1)} all-to-all(bf16[4,4,16,4096]{3,1,2,0:T(4,128)(2,1)S(1)} %copy.41), channel_id=1, replica_groups=mesh['groups'=2,'ep'=4,'tp'=4] {'ep'}, dimensions={0} | all-to-all | bytes 4194304 | tf_op jit(solution)/shard_map/all_to_all | solution.py:88
  87.5 1.2 copy.42
  88.6 2.0 convolution_bitcast_fusion.1
  90.6 13.7 %fusion.1 = bf16[1,4,64,4096]{3,2,1,0:T(8,128)(2,1)} fusion(bf16[4,384,4096]{2,1,0:T(8,128)(2,1)} %param.27, bf16[4,64,4096]{2,1,0:T(8,128)(2,1)S(1)} %bitcast.121, bf16[4,4096,384]{2,1,0:T(8,128)(2,1)} %param.26, f32[1,4,64,384]{3,2,1,0:T(8,128)S(1)} %convolution_bitcast_fusion.1), kind=kOutput, calls=%fused_computation.4 | convolution fusion | flops 1612251136 | bytes 29753344 | tf_op jit(solution)/shard_map/aesf,efd->aesd/dot_general | solution.py:97
  104.3 3.2 %copy.43 = bf16[1,4,64,4096]{3,1,0,2:T(4,128)(2,1)S(1)} copy(bf16[1,4,64,4096]{3,2,1,0:T(8,128)(2,1)} %fusion.1) | data formatting | bytes 4194304 | tf_op jit(solution)/shard_map/convert_element_type | solution.py:102
  107.5 50.3 %all_to_all.34 = bf16[1,4,64,4096]{3,1,0,2:T(4,128)(2,1)S(1)} all-to-all(bf16[1,4,64,4096]{3,1,0,2:T(4,128)(2,1)S(1)} %copy.43), channel_id=1, replica_groups=mesh['groups'=2,'ep'=4,'tp'=4] {'ep'}, dimensions={2} | all-to-all | bytes 4194304 | tf_op jit(solution)/shard_map/all_to_all | solution.py:103
  157.9 3.0 %copy.44 = bf16[4,4,4,4,4096]{4,3,1,0,2:T(4,128)(2,1)} copy(bf16[4,4,4,4,4096]{4,1,3,2,0:T(4,128)(2,1)S(1)} %bitcast.123) | data formatting | bytes 4194304 | tf_op jit(solution)/shard_map/all_to_all | solution.py:103
  161.0 0.5 copy-done.4
  161.6 0.6 dynamic-slice
  162.2 49.4 %all-reduce.3.cloned.1.call-done = bf16[4,4,4,4,4096]{4,3,1,0,2:T(4,128)(2,1)} async-done(((bf16[4,4,4,4,4096]{4,3,1,0,2:T(4,128)(2,1)}), bf16[4,4,4,4,4096]{4,3,1,0,2:T(4,128)(2,1)}) %all-reduce.3.cloned.1.call-update) | async-done | bytes 2097168
  211.6 1.8 dynamic-slice_convert_fusion
  213.4 0.4 reshape.137
  213.8 0.7 gather_fusion
  214.5 0.2 fusion.7
  214.7 0.7 fusion.24
  (27 shorter events, 1.0 us)
Async XLA Ops:
  7.2 4.5 %copy-start = (bf16[4,64,256]{2,1,0:T(8,128)(2,1)S(1)}, bf16[4,64,256]{2,1,0:T(8,128)(2,1)}, u32[]{:S(2)}) copy-start(bf16[4,64,256]{2,1,0:T(8,128)(2,1)} %param.17) | copy-start | bytes 393220
  7.2 204.4 %all-reduce.3.cloned.1.call-start = ((), (), s32[]{:S(2)}) async-start(), calls=%async_computation.2 | async-start | bytes 4194304
  31.0 57.7 %copy-start.1 = (bf16[4,4096,384]{2,1,0:T(8,128)(2,1)S(1)}, bf16[4,4096,384]{2,1,0:T(8,128)(2,1)}, u32[]{:S(2)}) copy-start(bf16[4,4096,384]{2,1,0:T(8,128)(2,1)} %param.25) | copy-start | bytes 37748740
  160.9 0.7 copy-start.4
  213.7 0.8 copy-start.3
  213.7 1.0 copy-start.2
Sparse Core Ops, SparseCore 0:
  161.1 50.4 all-reduce.2
where the time goes:
time: 223 us; the launch traced here: 222 us
  blocking collectives  116 us (52%)
  waiting for transfers between devices  49.4 us (22%)
  matrix products  18 us (8%)
  local copies, waits for them, and re-layouts  17.2 us (8%)
  between operations  14.2 us (6%)
  other arithmetic  7.48 us (3%)
    all_to_all x1, blocking collectives, local(): lax.all_to_all(placed_rows.reshape(ep_count, local_experts, tp_count * ca...  53.8 us
    all_to_all x1, blocking collectives, local(): lax.all_to_all(partial_value, 'ep', split_axis=2, concat_axis=0, tiled=True)  50.3 us
    unnamed x2, waiting for transfers between devices  49.4 us
    dot_general x1, matrix products, local(): jnp.einsum('aesf,efd->aesd', (jax.nn.silu(gate_act) * up_act).astype(jnp....  13.7 us
    all_gather x1, blocking collectives, local(): lax.all_gather(normed, 'tp', axis=0, tiled=True)  6.48 us
    all_gather x1, blocking collectives, local(): lax.all_gather(spread, 'tp', axis=0, tiled=True)  5.24 us
    reshape x2, local copies, waits for them, and re-layouts, local(): placed_rows.reshape(ep_count, local_experts, tp_count * capacity, width)  4.88 us
  transfers between devices with their start and end apart: 1, of which 1 were waited for; matrix products, arithmetic and copies ran while one was open for 0% of the time, Pallas kernels for 0%

commit v1 on v0

--- a/solution.py
+++ b/solution.py
@@ -50,8 +50,6 @@
     w_up,
     w_down,
 ):
-    tp_count = lax.axis_size("tp")
-    ep_count = lax.axis_size("ep")
     row_count = x_rows.shape[0]
     width = x_rows.shape[1]
     stream = x_rows.astype(jnp.float32) + attend(
@@ -61,53 +59,37 @@
     normed = (stream * scaled * norm_gain.astype(jnp.float32)).astype(jnp.bfloat16)
     experts_total = expert_place.shape[0]
     local_experts = w_gate.shape[0]
-    top_count = expert_ids.shape[1]
-    capacity = max(2, 2 * row_count * top_count // experts_total)
     expert_range = jnp.arange(experts_total, dtype=jnp.int32)
-    target = jnp.sum(
-        jnp.where(expert_ids[:, :, None] == expert_range, expert_place, 0), axis=2
-    ).reshape(-1)
-    hits = (target[:, None] == expert_range[None, :]).astype(jnp.int32)
-    earlier = jnp.sum((jnp.cumsum(hits, axis=0) - hits) * hits, axis=1)
-    slot_index = target * capacity + earlier
-    slot_range = jnp.arange(experts_total * capacity, dtype=jnp.int32)
-    spread = jnp.any(
-        slot_index.reshape(row_count, top_count)[:, :, None] == slot_range, axis=1
+    target = jnp.sum(jnp.where(expert_ids[:, :, None] == expert_range, expert_place, 0), axis=2)
+    table = jnp.sum(
+        jnp.where(target[:, :, None] == expert_range, gate_probs[:, :, None], 0.0), axis=1
+    )
+    high = lax.reduce_precision(table, 8, 7)
+    middle = lax.reduce_precision(table - high, 8, 7)
+    low = table - high - middle
+    pad = (-3 * experts_total) % 128
+    pieces = jnp.concatenate(
+        [high, middle, low, jnp.zeros((row_count, pad), jnp.float32)], axis=1
     ).astype(jnp.bfloat16)
-    group_rows, group_spread = (
-        lax.all_gather(normed, "tp", axis=0, tiled=True),
-        lax.all_gather(spread, "tp", axis=0, tiled=True),
+    gathered = lax.all_gather(
+        jnp.concatenate([normed, pieces], axis=1), ("ep", "tp"), axis=0, tiled=True
     )
-    layout = group_spread.reshape(tp_count, row_count, experts_total, capacity)
-    placed_rows = jnp.einsum(
-        "trjc,trd->jtcd",
-        layout,
-        group_rows.reshape(tp_count, row_count, width),
-        preferred_element_type=jnp.float32,
+    rows = gathered[:, :width]
+    sent = gathered[:, width : width + 3 * experts_total].astype(jnp.float32)
+    first = lax.axis_index("ep") * local_experts
+    parts = sent.reshape(-1, 3, experts_total)
+    weights = lax.dynamic_slice_in_dim(
+        parts[:, 0] + (parts[:, 1] + parts[:, 2]), first, local_experts, axis=1
+    )
+    gate_act = jnp.einsum("sd,edf->esf", rows, w_gate, preferred_element_type=jnp.float32)
+    up_act = jnp.einsum("sd,edf->esf", rows, w_up, preferred_element_type=jnp.float32)
+    hidden = (jax.nn.silu(gate_act) * up_act * weights.T[:, :, None]).astype(jnp.bfloat16)
+    partial_value = jnp.einsum(
+        "esf,efd->sd", hidden, w_down, preferred_element_type=jnp.float32
     ).astype(jnp.bfloat16)
-    arrived = lax.all_to_all(
-        placed_rows.reshape(ep_count, local_experts, tp_count * capacity, width),
-        "ep",
-        split_axis=0,
-        concat_axis=2,
-        tiled=True,
-    )
-    gate_act = jnp.einsum("aesd,edf->aesf", arrived, w_gate, preferred_element_type=jnp.float32)
-    up_act = jnp.einsum("aesd,edf->aesf", arrived, w_up, preferred_element_type=jnp.float32)
-    partial_value = jnp.einsum(
-        "aesf,efd->aesd",
-        (jax.nn.silu(gate_act) * up_act).astype(jnp.bfloat16),
-        w_down,
-        preferred_element_type=jnp.float32,
-    ).astype(jnp.bfloat16)
-    returned = lax.all_to_all(partial_value, "ep", split_axis=2, concat_axis=0, tiled=True)
-    terms = returned.astype(jnp.float32).reshape(ep_count, local_experts, tp_count, capacity, width)
-    own_slots = lax.psum_scatter(
-        terms.astype(jnp.bfloat16), "tp", scatter_dimension=2, tiled=True
+    mixed = lax.psum_scatter(
+        partial_value, ("ep", "tp"), scatter_dimension=0, tiled=True
     ).astype(jnp.float32)
-    own_slots = own_slots.reshape(experts_total * capacity, width)
-    chosen = own_slots[slot_index].reshape(row_count, top_count, width)
-    mixed = jnp.sum(chosen * gate_probs[:, :, None], axis=1)
     return ((stream + mixed).astype(jnp.bfloat16), mixed.astype(jnp.bfloat16))
 
 

time: 223 us -> 158 us (0.71)
  blocking collectives: 116 us -> 24.6 us
  waiting for transfers between devices: 49.4 us -> 86.3 us
  local copies, waits for them, and re-layouts: 17.2 us -> 3.07 us
  matrix products: 18 us -> 21.9 us
    all_to_all x2 -> x0, blocking collectives: 104 us -> none  [the longest x1 53.8 us: local(): lax.all_to_all(placed_rows.reshape(ep_count, local_experts, tp_count * ca...]
    unnamed x2, waiting for transfers between devices: 49.4 us -> 86.3 us
    all_gather x2 -> x1, blocking collectives: 11.7 us -> 24.6 us  [local(): lax.all_gather(jnp.concatenate([normed, pieces], axis=1), ('ep', 'tp'), a...]
    reshape x5 -> x0, local copies, waits for them, and re-layouts: 5.52 us -> none  [the longest x2 4.88 us: local(): placed_rows.reshape(ep_count, local_experts, tp_count * capacity, width)]
    all_to_all x2 -> x0, local copies, waits for them, and re-layouts: 4.18 us -> none  [the longest x1 3.02 us: local(): lax.all_to_all(partial_value, 'ep', split_axis=2, concat_axis=0, tiled=True)]
    dot_general x3 -> x2, matrix products: 16.5 us -> 20.3 us  [the longest x1 13.5 us: local(): jnp.einsum('esf,efd->sd', hidden, w_down, preferred_element_type=jnp.floa...]
    convert_element_type x1 -> x0, local copies, waits for them, and re-layouts: 3.21 us -> none  [local(): partial_value = jnp.einsum('aesf,efd->aesd', (jax.nn.silu(gate_act) * up_...]
where the time goes in v1:
time: 158 us; the launch traced here: 157 us
  waiting for transfers between devices  86.3 us (55%)
  blocking collectives  24.6 us (16%)
  matrix products  21.9 us (14%)
  between operations  14.8 us (9%)
  other arithmetic  6.68 us (4%)
  local copies, waits for them, and re-layouts  3.07 us (2%)
    unnamed x2, waiting for transfers between devices  86.3 us
    all_gather x1, blocking collectives, local(): lax.all_gather(jnp.concatenate([normed, pieces], axis=1), ('ep', 'tp'), a...  24.6 us
    dot_general x1, matrix products, local(): jnp.einsum('esf,efd->sd', hidden, w_down, preferred_element_type=jnp.floa...  13.5 us
    dot_general x1, matrix products, local(): jnp.einsum('sd,edf->esf', rows, w_gate, preferred_element_type=jnp.float32)  6.85 us
  transfers between devices with their start and end apart: 1, of which 1 were waited for; matrix products, arithmetic and copies ran while one was open for 0% of the time, Pallas kernels for 0%

profile of v1, /device:TPU:0, one launch (start us, length us, event | category | flops | bytes accessed | tf_op | source)
XLA Modules:
  0.0 157.4 jit_solution(16330732726497384786)
XLA Ops:
  7.2 0.0 copy-start
  7.2 0.0 all-reduce.3.cloned.1.call-start
  7.2 0.8 iota_compare_fusion.2
  8.0 0.8 copy.40
  8.8 0.7 reshape.79
  9.4 0.1 fusion.28
  9.6 1.2 fusion.27
  10.8 0.2 fusion.17
  11.0 0.7 reshape.69
  11.7 0.0 copy-done
  11.7 0.3 fusion.4
  12.0 0.9 multiply_reduce_fusion
  12.9 0.7 convert_element_type.30
  13.6 0.9 select_reduce_fusion.1
  14.5 0.8 select_reduce_fusion
  15.3 0.8 multiply_convert_fusion
  16.2 0.1 concatenate.6
  16.3 24.6 %all-gather = bf16[16,4,4224]{2,1,0:T(4,128)(2,1)S(1)} all-gather(bf16[1,4,4224]{2,1,0:T(4,128)(2,1)S(1)} %bitcast.69), channel_id=1, replica_groups=mesh['groups'=2,'ep'=4,'tp'=4] {'ep','tp'}, dimensions={0}, use_global_device_ids=true | all-gather | bytes 574464 | tf_op jit(solution)/shard_map/all_gather | solution.py:74
  40.9 0.1 reshape.73
  41.0 0.1 copy.37
  41.1 6.9 %convolution_bitcast_fusion.2 = f32[4,64,384]{2,1,0:T(8,128)S(1)} fusion(bf16[4,4096,384]{2,1,0:T(8,128)(2,1)} %param.25, bf16[64,4224]{1,0:T(8,128)(2,1)S(1)} %reshape.73), kind=kOutput, calls=%fused_computation.3 | convolution fusion | flops 805306368 | bytes 13500416 | tf_op jit(solution)/shard_map/sd,edf->esf/dot_general | solution.py:84
  48.0 0.0 copy-start.2
  48.0 0.0 copy-start.1
  48.0 13.5 %fusion = bf16[64,4096]{1,0:T(8,128)(2,1)} fusion(bf16[4,384,4096]{2,1,0:T(8,128)(2,1)} %param.27, bf16[4,4096,384]{2,1,0:T(8,128)(2,1)} %param.26, bf16[64,4224]{1,0:T(8,128)(2,1)S(1)} %reshape.73, f32[4,64,384]{2,1,0:T(8,128)S(1)} %convolution_bitcast_fusion.2, f32[4,64]{1,0:T(4,128)S(1)} %fusion.22), kind=kOutput, calls=%fused_computation.1 | convolution fusion | flops 1611563008 | bytes 26609664 | tf_op jit(solution)/shard_map/esf,efd->sd/dot_general | solution.py:87
  61.5 0.0 all-reduce.3.cloned.1.call-update
  61.5 0.0 copy-done.2
  61.6 0.6 dynamic-slice.1
  62.8 86.3 %all-reduce.3.cloned.1.call-done = bf16[64,4096]{1,0:T(8,128)(2,1)} async-done(((bf16[64,4096]{1,0:T(8,128)(2,1)}), bf16[64,4096]{1,0:T(8,128)(2,1)}) %all-reduce.3.cloned.1.call-update) | async-done | bytes 524304
  149.0 0.0 copy-done.1
  149.1 1.5 add_convert_fusion
  (8 shorter events, 0.1 us)
Async XLA Ops:
  7.2 4.5 %copy-start = (bf16[4,64,256]{2,1,0:T(8,128)(2,1)S(1)}, bf16[4,64,256]{2,1,0:T(8,128)(2,1)}, u32[]{:S(2)}) copy-start(bf16[4,64,256]{2,1,0:T(8,128)(2,1)} %param.17) | copy-start | bytes 393220
  7.2 141.9 %all-reduce.3.cloned.1.call-start = ((), (), s32[]{:S(2)}) async-start(), calls=%async_computation | async-start | bytes 1048576
  48.0 13.5 %copy-start.2 = (u32[32]{0:T(128)S(1)}, u32[32]{0:T(128)}, u32[]{:S(2)}) copy-start(u32[32]{0:T(128)} %constant.43) | copy-start | bytes 388
  48.0 101.0 %copy-start.1 = (bf16[4,4096]{1,0:T(4,128)(2,1)S(1)}, bf16[4,4096]{1,0:T(4,128)(2,1)}, u32[]{:S(2)}) copy-start(bf16[4,4096]{1,0:T(4,128)(2,1)} %param.14) | copy-start | bytes 98308
Sparse Core Ops, SparseCore 0:
  61.7 87.3 all-reduce.2

commit v2 on v1

--- a/solution.py
+++ b/solution.py
@@ -1,6 +1,10 @@
+import functools
+
 import jax
 import jax.numpy as jnp
 from jax import lax
+from jax.experimental import pallas as pl
+from jax.experimental.pallas import tpu as pltpu
 from jax.sharding import PartitionSpec as P
 
 HEAD_DIM = 128
@@ -32,6 +36,297 @@
     summed = jnp.einsum("rgjp,rpgd->rgjd", weights, cached_values, precision=highest)
     summed = summed + own_weight[..., None] * fresh_value[:, :, None, :]
     return (summed / denominator[..., None]).reshape(row_count, Q_HEADS * HEAD_DIM)
+
+
+CHUNKS = 4
+MESH = pl.DeviceIdType.MESH
+
+
+def flip(index, bit):
+    return index + bit - 2 * bit * lax.rem(lax.div(index, bit), 2)
+
+
+def low_bit(number):
+    return number & -number
+
+
+def experts_kernel(
+    n_ep,
+    n_tp,
+    message_ref,
+    stream_ref,
+    w_gate,
+    w_up,
+    w_down,
+    out_ref,
+    mix_ref,
+    gate_v,
+    up_v,
+    down_v,
+    arrived,
+    rows,
+    hidden,
+    sums,
+    sent,
+    taken,
+    packed_wide,
+    packed,
+    back,
+    weight_sem,
+    ep_send,
+    ep_recv,
+    tp_send,
+    tp_recv,
+    sum_send,
+    sum_recv,
+    back_send,
+    back_recv,
+):
+    experts, width, units = gate_v.shape
+    row_count = stream_ref.shape[0]
+    block = n_ep * row_count
+    part = width // row_count
+    span = width // CHUNKS
+    piece = span // row_count
+    bits = []
+    bit = n_tp // 2
+    while bit:
+        bits.append(bit)
+        bit //= 2
+    me_ep = lax.axis_index("ep")
+    me_tp = lax.axis_index("tp")
+
+    loads = []
+    for e in range(experts):
+        for k, (source, target) in enumerate(((w_gate, gate_v), (w_up, up_v))):
+            loads.append(
+                pltpu.make_async_copy(source.at[e], target.at[e], weight_sem.at[2 * e + k])
+            )
+    down_load = pltpu.make_async_copy(w_down, down_v, weight_sem.at[2 * experts])
+    for load in loads:
+        load.start()
+    down_load.start()
+
+    arrived[0, 0] = message_ref[...]
+    barrier = pltpu.get_barrier_semaphore()
+    for j in range(1, n_ep):
+        pl.semaphore_signal(
+            barrier, inc=1, device_id={"ep": lax.rem(me_ep + j, n_ep)}, device_id_type=MESH
+        )
+    for b in bits:
+        pl.semaphore_signal(barrier, inc=1, device_id={"tp": flip(me_tp, b)}, device_id_type=MESH)
+    pl.semaphore_wait(barrier, n_ep - 1 + len(bits))
+
+    sends = []
+    along = {}
+    for j in range(1, n_ep):
+        s = n_ep - j
+        along[s] = pltpu.make_async_remote_copy(
+            src_ref=arrived.at[0, 0],
+            dst_ref=arrived.at[0, s],
+            send_sem=ep_send.at[s],
+            recv_sem=ep_recv.at[s],
+            device_id={"ep": lax.rem(me_ep + j, n_ep)},
+            device_id_type=MESH,
+        )
+        along[s].start()
+        sends.append(along[s])
+    across = {}
+    order = [0] + [s for d in range(1, n_ep) for s in (d, n_ep - d) if d <= s]
+    order = list(dict.fromkeys(order))
+    for m in range(n_tp):
+        for s in order:
+            if m:
+                across[m, s].wait_recv()
+            elif s:
+                along[s].wait_recv()
+            for b in bits:
+                if m == 0 or b < low_bit(m):
+                    copy = pltpu.make_async_remote_copy(
+                        src_ref=arrived.at[m, s],
+                        dst_ref=arrived.at[m | b, s],
+                        send_sem=tp_send.at[m | b, s],
+                        recv_sem=tp_recv.at[m | b, s],
+                        device_id={"tp": flip(me_tp, b)},
+                        device_id_type=MESH,
+                    )
+                    copy.start()
+                    across[m | b, s] = copy
+                    sends.append(copy)
+
+    group = row_count * row_count
+    to = lax.broadcasted_iota(jnp.int32, (block, n_ep * group), 0)
+    source = lax.broadcasted_iota(jnp.int32, (block, n_ep * group), 1)
+    tables = []
+    for m in range(n_tp):
+        held = arrived[m].reshape(n_ep * group, part + 128)
+        table = jnp.zeros((block, 128), jnp.float32)
+        for q in range(row_count):
+            wanted = lax.div(to, row_count) * group + q * row_count + lax.rem(to, row_count)
+            pick = jnp.where(source == wanted, 1.0, 0.0).astype(jnp.bfloat16)
+            moved = jnp.dot(pick, held, preferred_element_type=jnp.float32)
+            rows[m * block : (m + 1) * block, q * part : (q + 1) * part] = moved[:, :part].astype(
+                jnp.bfloat16
+            )
+            table = table + moved[:, part:]
+        tables.append(table)
+    table = jnp.concatenate(tables, axis=0)
+    lane = lax.broadcasted_iota(jnp.int32, table.shape, 1)
+
+    for e in range(experts):
+        loads[2 * e].wait()
+        gate = jnp.dot(rows[...], gate_v[e], preferred_element_type=jnp.float32)
+        loads[2 * e + 1].wait()
+        up = jnp.dot(rows[...], up_v[e], preferred_element_type=jnp.float32)
+        share = jnp.sum(
+            jnp.where(lane == me_ep * experts + e, table, 0.0), axis=1, keepdims=True
+        )
+        act = gate / (1.0 + jnp.exp(-gate)) * up * share
+        hidden[:, e * units : (e + 1) * units] = act.astype(jnp.bfloat16)
+    down_load.wait()
+
+    summing = {}
+    returning = {}
+
+    def columns(c):
+        return slice(c * span, (c + 1) * span)
+
+    def send_sums(c, b):
+        for m in range(1, n_tp):
+            if low_bit(m) == b:
+                if b > 1:
+                    sent[c, m] = sums[m // 2, :, columns(c)].astype(jnp.bfloat16)
+                copy = pltpu.make_async_remote_copy(
+                    src_ref=sent.at[c, m],
+                    dst_ref=taken.at[c, m],
+                    send_sem=sum_send.at[c, m],
+                    recv_sem=sum_recv.at[c, m],
+                    device_id={"tp": flip(me_tp, b)},
+                    device_id_type=MESH,
+                )
+                copy.start()
+                summing[c, m] = copy
+                sends.append(copy)
+
+    def take_sums(c, b):
+        for m in range(1, n_tp):
+            if low_bit(m) == b:
+                summing[c, m].wait_recv()
+                sums[(m - b) // 2, :, columns(c)] += taken[c, m].astype(jnp.float32)
+
+    def send_back(c):
+        for s in range(n_ep):
+            for q in range(row_count):
+                packed_wide[c, s, q * row_count : (q + 1) * row_count, :] = sums[
+                    0,
+                    s * row_count : (s + 1) * row_count,
+                    c * span + q * piece : c * span + (q + 1) * piece,
+                ]
+            if s:
+                packed[c, s] = packed_wide[c, s].astype(jnp.bfloat16)
+                copy = pltpu.make_async_remote_copy(
+                    src_ref=packed.at[c, s],
+                    dst_ref=back.at[c, n_ep - s],
+                    send_sem=back_send.at[c, n_ep - s],
+                    recv_sem=back_recv.at[c, n_ep - s],
+                    device_id={"ep": lax.rem(me_ep + s, n_ep)},
+                    device_id_type=MESH,
+                )
+                copy.start()
+                returning[c, s] = copy
+                sends.append(copy)
+
+    def compute(c):
+        product = jnp.dot(hidden[...], down_v[:, columns(c)], preferred_element_type=jnp.float32)
+        for m in range(n_tp):
+            mine = product[m * block : (m + 1) * block]
+            if m % 2:
+                sent[c, m] = mine.astype(jnp.bfloat16)
+            else:
+                sums[m // 2, :, columns(c)] = mine
+        if bits:
+            send_sums(c, 1)
+        else:
+            send_back(c)
+
+    def turn(c, k):
+        b = 1 << k
+        take_sums(c, b)
+        if 2 * b < n_tp:
+            send_sums(c, 2 * b)
+        else:
+            send_back(c)
+
+    def finish(c):
+        total = packed_wide[c, 0]
+        for s in range(1, n_ep):
+            returning[c, s].wait_recv()
+            total = total + back[c, n_ep - s].astype(jnp.float32)
+        packed_wide[c, 0] = total
+        for q in range(row_count):
+            place = slice(c * span + q * piece, c * span + (q + 1) * piece)
+            mixed = packed_wide[c, 0, q * row_count : (q + 1) * row_count, :]
+            mix_ref[:, place] = mixed.astype(jnp.bfloat16)
+            out_ref[:, place] = (stream_ref[:, place] + mixed).astype(jnp.bfloat16)
+
+    stages = [compute] + [functools.partial(turn, k=k) for k in range(len(bits))] + [finish]
+    for time in range(CHUNKS + len(stages) - 1):
+        for k, stage in enumerate(stages):
+            if 0 <= time - k < CHUNKS:
+                stage(time - k)
+    for copy in sends:
+        copy.wait_send()
+
+
+def run_experts(message, stream, w_gate, w_up, w_down):
+    n_ep, n_tp = lax.axis_size("ep"), lax.axis_size("tp")
+    experts, width, units = w_gate.shape
+    row_count = stream.shape[0]
+    group = row_count * row_count
+    block = n_ep * row_count
+    span = width // CHUNKS
+    bf16, f32 = jnp.bfloat16, jnp.float32
+    vmem = pl.BlockSpec(memory_space=pltpu.VMEM)
+    hbm = pl.BlockSpec(memory_space=pl.ANY)
+    dma = pltpu.SemaphoreType.DMA
+    result = jax.ShapeDtypeStruct((row_count, width), bf16)
+    all_rows = n_tp * block
+    weight_count = 3 * experts * width * units
+    return pl.pallas_call(
+        functools.partial(experts_kernel, n_ep, n_tp),
+        out_shape=(result, result),
+        in_specs=[vmem, vmem, hbm, hbm, hbm],
+        out_specs=(vmem, vmem),
+        scratch_shapes=[
+            pltpu.VMEM((experts, width, units), bf16),
+            pltpu.VMEM((experts, width, units), bf16),
+            pltpu.VMEM((experts * units, width), bf16),
+            pltpu.VMEM((n_tp, n_ep, group, width // row_count + 128), bf16),
+            pltpu.VMEM((all_rows, width), bf16),
+            pltpu.VMEM((all_rows, experts * units), bf16),
+            pltpu.VMEM(((n_tp + 1) // 2, block, width), f32),
+            pltpu.VMEM((CHUNKS, n_tp, block, span), bf16),
+            pltpu.VMEM((CHUNKS, n_tp, block, span), bf16),
+            pltpu.VMEM((CHUNKS, n_ep, group, span // row_count), f32),
+            pltpu.VMEM((CHUNKS, n_ep, group, span // row_count), bf16),
+            pltpu.VMEM((CHUNKS, n_ep, group, span // row_count), bf16),
+            dma((2 * experts + 1,)),
+            dma((n_ep,)),
+            dma((n_ep,)),
+            dma((n_tp, n_ep)),
+            dma((n_tp, n_ep)),
+            dma((CHUNKS, n_tp)),
+            dma((CHUNKS, n_tp)),
+            dma((CHUNKS, n_ep)),
+            dma((CHUNKS, n_ep)),
+        ],
+        compiler_params=pltpu.CompilerParams(
+            collective_id=0, has_side_effects=True, vmem_limit_bytes=60 * 2**20
+        ),
+        cost_estimate=pl.CostEstimate(
+            flops=2 * all_rows * weight_count, bytes_accessed=2 * weight_count, transcendentals=0
+        ),
+    )(message, stream, w_gate, w_up, w_down.reshape(experts * units, width))
 
 
 def local(
@@ -58,7 +353,6 @@
     scaled = lax.rsqrt(jnp.mean(stream * stream, axis=1, keepdims=True) + 1e-06)
     normed = (stream * scaled * norm_gain.astype(jnp.float32)).astype(jnp.bfloat16)
     experts_total = expert_place.shape[0]
-    local_experts = w_gate.shape[0]
     expert_range = jnp.arange(experts_total, dtype=jnp.int32)
     target = jnp.sum(jnp.where(expert_ids[:, :, None] == expert_range, expert_place, 0), axis=2)
     table = jnp.sum(
@@ -67,30 +361,13 @@
     high = lax.reduce_precision(table, 8, 7)
     middle = lax.reduce_precision(table - high, 8, 7)
     low = table - high - middle
-    pad = (-3 * experts_total) % 128
-    pieces = jnp.concatenate(
-        [high, middle, low, jnp.zeros((row_count, pad), jnp.float32)], axis=1
-    ).astype(jnp.bfloat16)
-    gathered = lax.all_gather(
-        jnp.concatenate([normed, pieces], axis=1), ("ep", "tp"), axis=0, tiled=True
+    pieces = jnp.stack([high, middle, low], axis=0).astype(jnp.bfloat16)
+    pieces = jnp.pad(pieces, ((0, row_count - 3), (0, 0), (0, 128 - experts_total)))
+    quarters = normed.reshape(row_count, row_count, width // row_count).transpose(1, 0, 2)
+    message = jnp.concatenate([quarters, pieces], axis=2).reshape(
+        row_count * row_count, width // row_count + 128
     )
-    rows = gathered[:, :width]
-    sent = gathered[:, width : width + 3 * experts_total].astype(jnp.float32)
-    first = lax.axis_index("ep") * local_experts
-    parts = sent.reshape(-1, 3, experts_total)
-    weights = lax.dynamic_slice_in_dim(
-        parts[:, 0] + (parts[:, 1] + parts[:, 2]), first, local_experts, axis=1
-    )
-    gate_act = jnp.einsum("sd,edf->esf", rows, w_gate, preferred_element_type=jnp.float32)
-    up_act = jnp.einsum("sd,edf->esf", rows, w_up, preferred_element_type=jnp.float32)
-    hidden = (jax.nn.silu(gate_act) * up_act * weights.T[:, :, None]).astype(jnp.bfloat16)
-    partial_value = jnp.einsum(
-        "esf,efd->sd", hidden, w_down, preferred_element_type=jnp.float32
-    ).astype(jnp.bfloat16)
-    mixed = lax.psum_scatter(
-        partial_value, ("ep", "tp"), scatter_dimension=0, tiled=True
-    ).astype(jnp.float32)
-    return ((stream + mixed).astype(jnp.bfloat16), mixed.astype(jnp.bfloat16))
+    return run_experts(message, stream, w_gate, w_up, w_down)
 
 
 def solution(mesh):

time: 158 us -> 50.7 us (0.32)
  waiting for transfers between devices: 86.3 us -> 0 us
  Pallas kernels: 0 us -> 37.7 us
  blocking collectives: 24.6 us -> 0 us
  matrix products: 21.9 us -> 1.57 us
  between operations: 14.8 us -> 0.72 us
  local copies, waits for them, and re-layouts: 3.07 us -> 5.62 us
  other arithmetic: 6.68 us -> 4.44 us
    unnamed x2 -> x0, waiting for transfers between devices: 86.3 us -> none
    pallas_call x0 -> x1, Pallas kernels: none -> 37.7 us  [run_experts(): pl.pallas_call(functools.partial(experts_kernel, n_ep, n_tp), out_shape=(...]
    all_gather x1 -> x0, blocking collectives: 24.6 us -> none  [local(): lax.all_gather(jnp.concatenate([normed, pieces], axis=1), ('ep', 'tp'), a...]
    dot_general x2 -> x0, matrix products: 20.3 us -> none  [the longest x1 13.5 us: local(): jnp.einsum('esf,efd->sd', hidden, w_down, preferred_element_type=jnp.floa...]
    unnamed x10 -> x8, local copies, waits for them, and re-layouts: 1.58 us -> 3.55 us
  transfers between devices with their start and end apart: 1 -> 0, of which waited for: 1 -> 0; matrix products, arithmetic and copies ran while one was open for 0% -> 0% of each run, Pallas kernels for 0% -> 0%
where the time goes in v2:
time: 50.7 us; the launch traced here: 50 us
  Pallas kernels  37.7 us (74%)
  local copies, waits for them, and re-layouts  5.62 us (11%)
  other arithmetic  4.44 us (9%)
  matrix products  1.57 us (3%)
  between operations  0.72 us (1%)
    pallas_call x1, Pallas kernels, run_experts(): pl.pallas_call(functools.partial(experts_kernel, n_ep, n_tp), out_shape=(...  37.7 us
    unnamed x8, local copies, waits for them, and re-layouts  3.55 us
    dot_general x1, matrix products, attend(): jnp.einsum('rgjd,rpgd->rgjp', query, cached_keys, precision=highest)  1.15 us

profile of v2, /device:TPU:0, one launch (start us, length us, event | category | flops | bytes accessed | tf_op | source)
XLA Modules:
  0.0 50.0 jit_solution(11015234778861100446)
XLA Ops:
  0.6 0.0 copy-start
  0.6 0.8 %iota_compare_fusion.3 = pred[4,64]{1,0:T(4,128)(4,1)S(1)} fusion(s32[4]{0:T(128)} %param.20), kind=kLoop, calls=%fused_computation.31 | loop fusion | flops 256 | bytes 272 | tf_op jit(solution)/shard_map/lt | solution.py:30
  1.4 0.8 %copy.29 = bf16[1,4,32,128]{3,2,1,0:T(8,128)(2,1)S(1)} copy(bf16[1,4,32,128]{3,1,2,0:T(4,128)(2,1)} %bitcast.43) | data formatting | bytes 65536
  2.2 1.2 %fusion.15 = (f32[4,2,16]{2,1,0:T(2,128)S(1)}, f32[4,2,16,64]{3,2,1,0:T(8,128)S(1)}) fusion(bf16[4,2,16,128]{3,2,1,0:T(8,128)(2,1)S(1)} %bitcast.39, pred[4,64]{1,0:T(4,128)(4,1)S(1)} %iota_compare_fusion.3, bf16[4,64,256]{2,1,0:T(8,128)(2,1)} %param.16), kind=kOutput, calls=%fused_computation.35 | convolution fusion | flops 2121600 | bytes 197376 | tf_op jit(solution)/shard_map/rgjd,rpgd->rgjp/dot_general | solution.py:28
  3.3 0.7 %reshape.97 = bf16[4,2,128,1]{2,3,1,0:T(2,128)(2,1)S(1)} reshape(bf16[4,256]{1,0:T(4,128)(2,1)} %param.18) | data formatting | bytes 4096 | tf_op jit(solution)/shard_map/reshape | solution.py:26
  4.0 0.1 fusion.16
  4.2 0.2 fusion.7
  4.4 0.7 %reshape.93 = f32[4,2,128]{2,1,0:T(2,128)S(1)} reshape(bf16[4,256]{1,0:T(4,128)(2,1)} %param.19) | data formatting | bytes 6144 | tf_op jit(solution)/shard_map/mul | solution.py:37
  5.1 0.0 copy-done
  5.1 0.3 fusion
  5.4 0.9 %multiply_reduce_fusion = (f32[4]{0:T(128)S(1)}, f32[4,4096]{1,0:T(4,128)S(1)}) fusion(f32[1,4,32,128]{3,2,1,0:T(8,128)S(1)} %bitcast.42, bf16[4,4096]{1,0:T(4,128)(2,1)} %param.14), kind=kLoop, calls=%fused_computation.12 | loop fusion | flops 65532 | bytes 163856 | tf_op jit(solution)/shard_map/reduce_sum | solution.py:353
  6.3 0.0 copy-start.1
  6.3 0.7 %convert_element_type.8 = f32[4096]{0:T(1024)S(1)} convert(bf16[4096]{0:T(1024)(128)(2,1)} %param.21) | non-fusion elementwise | flops 4096 | bytes 24576 | tf_op jit(solution)/shard_map/convert_element_type | solution.py:354
  7.1 0.1 multiply_convert_fusion
  7.2 0.9 %select_reduce_fusion.1 = s32[4,8]{1,0:T(4,128)S(1)} fusion(s32[16]{0:T(128)} %param.24, s32[4,8]{1,0:T(4,128)} %param.22), kind=kLoop, calls=%fused_computation.21 | loop fusion | flops 1504 | bytes 320 | tf_op jit(solution)/shard_map/reduce_sum | solution.py:357
  8.1 0.8 %select_reduce_fusion = f32[4,16]{1,0:T(4,128)S(1)} fusion(f32[4,8]{1,0:T(4,128)} %param.23, s32[4,8]{1,0:T(4,128)S(1)} %select_reduce_fusion.1), kind=kLoop, calls=%fused_computation.19 | loop fusion | flops 1472 | bytes 512 | tf_op jit(solution)/shard_map/reduce_sum | solution.py:358
  9.0 0.6 %reshape.91.message_ref = bf16[16,1152]{1,0:T(8,128)(2,1)} reshape(bf16[4,4,1152]{2,1,0:T(4,128)(2,1)S(1)} %copy.23) | data formatting | bytes 73728 | tf_op jit(solution)/shard_map/reshape | solution.py:367
  9.6 0.0 copy-done.1
  9.6 37.7 %shard_map.149 = (bf16[4,4096]{1,0:T(4,128)(2,1)}, bf16[4,4096]{1,0:T(4,128)(2,1)}) custom-call(bf16[16,1152]{1,0:T(8,128)(2,1)} %reshape.91.message_ref, f32[4,4096]{1,0:T(4,128)} %copy-done.1, bf16[4,4096,384]{2,1,0:T(8,128)(2,1)} %w_gate.1, bf16[4,4096,384]{2,1,0:T(8,128)(2,1)} %w_up.1, bf16[1536,4096]{1,0:T(8,128)(2,1)} %bitcast.38), custom_call_target="tpu_custom_call" | custom-call | flops 2415919104 | bytes 37748736 | tf_op jit(solution)/shard_map/pallas_call | solution.py:295
  47.3 1.4 %copy.45 = bf16[4,4096]{1,0:T(4,128)(2,1)} copy(bf16[4,4096]{1,0:T(4,128)(2,1)} %get-tuple-element.13) | data formatting | bytes 65536
  48.7 1.4 %copy.46 = bf16[4,4096]{1,0:T(4,128)(2,1)} copy(bf16[4,4096]{1,0:T(4,128)(2,1)} %get-tuple-element.14) | data formatting | bytes 65536
  (9 shorter events, 0.1 us)
Async XLA Ops:
  0.6 4.5 %copy-start = (bf16[4,64,256]{2,1,0:T(8,128)(2,1)S(1)}, bf16[4,64,256]{2,1,0:T(8,128)(2,1)}, u32[]{:S(2)}) copy-start(bf16[4,64,256]{2,1,0:T(8,128)(2,1)} %param.17) | copy-start | bytes 393220
  6.3 3.3 %copy-start.1 = (f32[4,4096]{1,0:T(4,128)}, f32[4,4096]{1,0:T(4,128)S(1)}, u32[]{:S(2)}) copy-start(f32[4,4096]{1,0:T(4,128)S(1)} %get-tuple-element.3.stream_ref) | copy-start | bytes 196612

commit v3 on v2

--- a/solution.py
+++ b/solution.py
@@ -12,32 +12,6 @@
 KV_HEADS = 2
 
 
-highest = lax.Precision.HIGHEST
-
-
-def attend(queries, key_cache, value_cache, new_key, new_value, lengths):
-    row_count = queries.shape[0]
-    span = key_cache.shape[1]
-    groups = Q_HEADS // KV_HEADS
-    factor = HEAD_DIM ** (-0.5)
-    query = queries.astype(jnp.float32).reshape(row_count, KV_HEADS, groups, HEAD_DIM)
-    cached_keys = key_cache.astype(jnp.float32).reshape(row_count, span, KV_HEADS, HEAD_DIM)
-    cached_values = value_cache.astype(jnp.float32).reshape(row_count, span, KV_HEADS, HEAD_DIM)
-    fresh_key = new_key.astype(jnp.float32).reshape(row_count, KV_HEADS, HEAD_DIM)
-    fresh_value = new_value.astype(jnp.float32).reshape(row_count, KV_HEADS, HEAD_DIM)
-    scores = jnp.einsum("rgjd,rpgd->rgjp", query, cached_keys, precision=highest) * factor
-    own_score = jnp.einsum("rgjd,rgd->rgj", query, fresh_key, precision=highest) * factor
-    valid = (jnp.arange(span, dtype=jnp.int32)[None, :] < lengths[:, None])[:, None, None, :]
-    masked = jnp.where(valid, scores, -1e30)
-    peak_all = jnp.maximum(jnp.max(masked, axis=3), own_score)
-    weights = jnp.where(valid, jnp.exp(masked - peak_all[..., None]), 0.0)
-    own_weight = jnp.exp(own_score - peak_all)
-    denominator = jnp.sum(weights, axis=3) + own_weight
-    summed = jnp.einsum("rgjp,rpgd->rgjd", weights, cached_values, precision=highest)
-    summed = summed + own_weight[..., None] * fresh_value[:, :, None, :]
-    return (summed / denominator[..., None]).reshape(row_count, Q_HEADS * HEAD_DIM)
-
-
 CHUNKS = 4
 MESH = pl.DeviceIdType.MESH
 
@@ -48,18 +22,101 @@
 
 def low_bit(number):
     return number & -number
+
+
+def attend(
+    x_ref, query_ref, key_ref, value_ref, new_key_ref, new_value_ref, length_ref, heads, stream
+):
+    row_count, span = key_ref.shape[0], key_ref.shape[1]
+    each = Q_HEADS // KV_HEADS
+    factor = HEAD_DIM ** (-0.5)
+    for h in range(Q_HEADS):
+        heads[:, h, :] = query_ref[:, h * HEAD_DIM : (h + 1) * HEAD_DIM].astype(jnp.float32)
+    position = lax.broadcasted_iota(jnp.int32, (each, span), 1)
+    for r in range(row_count):
+        valid = position < length_ref[r]
+        for g in range(KV_HEADS):
+            lanes = slice(g * HEAD_DIM, (g + 1) * HEAD_DIM)
+            own_rows = slice(g * each, (g + 1) * each)
+            query = heads[r, own_rows, :]
+            scores = factor * lax.dot_general(
+                query.astype(jnp.bfloat16),
+                key_ref[r, :, lanes],
+                (((1,), (1,)), ((), ())),
+                preferred_element_type=jnp.float32,
+            )
+            fresh_key = new_key_ref[:, lanes].astype(jnp.float32)[r : r + 1]
+            fresh_value = new_value_ref[:, lanes].astype(jnp.float32)[r : r + 1]
+            own = factor * jnp.sum(query * fresh_key, axis=1, keepdims=True)
+            masked = jnp.where(valid, scores, -1e30)
+            peak = jnp.maximum(jnp.max(masked, axis=1, keepdims=True), own)
+            weight = jnp.where(valid, jnp.exp(masked - peak), 0.0)
+            own_weight = jnp.exp(own - peak)
+            total = jnp.sum(weight, axis=1, keepdims=True) + own_weight
+            coarse = weight.astype(jnp.bfloat16)
+            fine = (weight - coarse.astype(jnp.float32)).astype(jnp.bfloat16)
+            value = value_ref[r, :, lanes]
+            summed = jnp.dot(coarse, value, preferred_element_type=jnp.float32)
+            summed = summed + jnp.dot(fine, value, preferred_element_type=jnp.float32)
+            heads[r, own_rows, :] = (summed + own_weight * fresh_value) / total
+    for h in range(Q_HEADS):
+        lanes = slice(h * HEAD_DIM, (h + 1) * HEAD_DIM)
+        stream[:, lanes] = x_ref[:, lanes].astype(jnp.float32) + heads[:, h, :]
+
+
+def pack(stream, gain_ref, ids_ref, prob_ref, place_ref, wide):
+    row_count, width = stream.shape
+    part = width // row_count
+    experts_total = place_ref.shape[1]
+    rows = stream[...]
+    scaled = lax.rsqrt(jnp.mean(rows * rows, axis=1, keepdims=True) + 1e-06)
+    normed = rows * scaled * gain_ref[...].astype(jnp.float32)
+    lane = lax.broadcasted_iota(jnp.int32, (row_count, 128), 1)
+    ids, probs = ids_ref[...], prob_ref[...]
+    table = jnp.zeros((row_count, 128), jnp.float32)
+    for k in range(ids.shape[1]):
+        table = table + jnp.where(lane == ids[:, k : k + 1], probs[:, k : k + 1], 0.0)
+    high = table.astype(jnp.bfloat16).astype(jnp.float32)
+    middle = (table - high).astype(jnp.bfloat16).astype(jnp.float32)
+    terms = [high, middle, table - high - middle]
+    wide[:, part:] = jnp.zeros((row_count * row_count, 128), jnp.float32)
+    for q in range(row_count):
+        wide[q * row_count : (q + 1) * row_count, :part] = normed[:, q * part : (q + 1) * part]
+        if q < len(terms):
+            wide[q * row_count : (q + 1) * row_count, part:] = terms[q]
+    slot = lax.broadcasted_iota(jnp.int32, (128, experts_total), 0)
+    placed = jnp.where(slot == place_ref[...], 1.0, 0.0).astype(jnp.bfloat16)
+    wide[:, part:] = lax.dot_general(
+        wide[:, part : part + experts_total].astype(jnp.bfloat16),
+        placed,
+        (((1,), (1,)), ((), ())),
+        preferred_element_type=jnp.float32,
+    )
+    return wide[...].astype(jnp.bfloat16)
 
 
 def experts_kernel(
     n_ep,
     n_tp,
-    message_ref,
-    stream_ref,
+    x_ref,
+    query_ref,
+    key_ref,
+    value_ref,
+    new_key_ref,
+    new_value_ref,
+    length_ref,
+    gain_ref,
+    ids_ref,
+    prob_ref,
+    place_ref,
     w_gate,
     w_up,
     w_down,
     out_ref,
     mix_ref,
+    heads,
+    stream_ref,
+    wide,
     gate_v,
     up_v,
     down_v,
@@ -107,7 +164,6 @@
         load.start()
     down_load.start()
 
-    arrived[0, 0] = message_ref[...]
     barrier = pltpu.get_barrier_semaphore()
     for j in range(1, n_ep):
         pl.semaphore_signal(
@@ -115,6 +171,10 @@
         )
     for b in bits:
         pl.semaphore_signal(barrier, inc=1, device_id={"tp": flip(me_tp, b)}, device_id_type=MESH)
+    attend(
+        x_ref, query_ref, key_ref, value_ref, new_key_ref, new_value_ref, length_ref, heads, stream_ref
+    )
+    arrived[0, 0] = pack(stream_ref, gain_ref, ids_ref, prob_ref, place_ref, wide)
     pl.semaphore_wait(barrier, n_ep - 1 + len(bits))
 
     sends = []
@@ -195,10 +255,10 @@
         for m in range(1, n_tp):
             if low_bit(m) == b:
                 if b > 1:
-                    sent[c, m] = sums[m // 2, :, columns(c)].astype(jnp.bfloat16)
+                    sent[c, m - 1] = sums[m // 2, :, columns(c)].astype(jnp.bfloat16)
                 copy = pltpu.make_async_remote_copy(
-                    src_ref=sent.at[c, m],
-                    dst_ref=taken.at[c, m],
+                    src_ref=sent.at[c, m - 1],
+                    dst_ref=taken.at[c, m - 1],
                     send_sem=sum_send.at[c, m],
                     recv_sem=sum_recv.at[c, m],
                     device_id={"tp": flip(me_tp, b)},
@@ -212,7 +272,7 @@
         for m in range(1, n_tp):
             if low_bit(m) == b:
                 summing[c, m].wait_recv()
-                sums[(m - b) // 2, :, columns(c)] += taken[c, m].astype(jnp.float32)
+                sums[(m - b) // 2, :, columns(c)] += taken[c, m - 1].astype(jnp.float32)
 
     def send_back(c):
         for s in range(n_ep):
@@ -241,7 +301,7 @@
         for m in range(n_tp):
             mine = product[m * block : (m + 1) * block]
             if m % 2:
-                sent[c, m] = mine.astype(jnp.bfloat16)
+                sent[c, m - 1] = mine.astype(jnp.bfloat16)
             else:
                 sums[m // 2, :, columns(c)] = mine
         if bits:
@@ -266,8 +326,8 @@
         for q in range(row_count):
             place = slice(c * span + q * piece, c * span + (q + 1) * piece)
             mixed = packed_wide[c, 0, q * row_count : (q + 1) * row_count, :]
-            mix_ref[:, place] = mixed.astype(jnp.bfloat16)
-            out_ref[:, place] = (stream_ref[:, place] + mixed).astype(jnp.bfloat16)
+            mix_ref[:, place] = mixed
+            out_ref[:, place] = stream_ref[:, place] + mixed
 
     stages = [compute] + [functools.partial(turn, k=k) for k in range(len(bits))] + [finish]
     for time in range(CHUNKS + len(stages) - 1):
@@ -278,10 +338,25 @@
         copy.wait_send()
 
 
-def run_experts(message, stream, w_gate, w_up, w_down):
+def local(
+    x_rows,
+    queries,
+    key_cache,
+    value_cache,
+    new_key,
+    new_value,
+    lengths,
+    norm_gain,
+    expert_ids,
+    gate_probs,
+    expert_place,
+    w_gate,
+    w_up,
+    w_down,
+):
     n_ep, n_tp = lax.axis_size("ep"), lax.axis_size("tp")
     experts, width, units = w_gate.shape
-    row_count = stream.shape[0]
+    row_count = x_rows.shape[0]
     group = row_count * row_count
     block = n_ep * row_count
     span = width // CHUNKS
@@ -289,15 +364,19 @@
     vmem = pl.BlockSpec(memory_space=pltpu.VMEM)
     hbm = pl.BlockSpec(memory_space=pl.ANY)
     dma = pltpu.SemaphoreType.DMA
-    result = jax.ShapeDtypeStruct((row_count, width), bf16)
+    smem = pl.BlockSpec(memory_space=pltpu.SMEM)
+    result = jax.ShapeDtypeStruct((row_count, width), f32)
     all_rows = n_tp * block
     weight_count = 3 * experts * width * units
-    return pl.pallas_call(
+    layer_out, mixed = pl.pallas_call(
         functools.partial(experts_kernel, n_ep, n_tp),
         out_shape=(result, result),
-        in_specs=[vmem, vmem, hbm, hbm, hbm],
+        in_specs=[vmem] * 6 + [smem] + [vmem] * 4 + [hbm] * 3,
         out_specs=(vmem, vmem),
         scratch_shapes=[
+            pltpu.VMEM((row_count, Q_HEADS, HEAD_DIM), f32),
+            pltpu.VMEM((row_count, width), f32),
+            pltpu.VMEM((group, width // row_count + 128), f32),
             pltpu.VMEM((experts, width, units), bf16),
             pltpu.VMEM((experts, width, units), bf16),
             pltpu.VMEM((experts * units, width), bf16),
@@ -305,8 +384,8 @@
             pltpu.VMEM((all_rows, width), bf16),
             pltpu.VMEM((all_rows, experts * units), bf16),
             pltpu.VMEM(((n_tp + 1) // 2, block, width), f32),
-            pltpu.VMEM((CHUNKS, n_tp, block, span), bf16),
-            pltpu.VMEM((CHUNKS, n_tp, block, span), bf16),
+            pltpu.VMEM((CHUNKS, max(n_tp - 1, 1), block, span), bf16),
+            pltpu.VMEM((CHUNKS, max(n_tp - 1, 1), block, span), bf16),
             pltpu.VMEM((CHUNKS, n_ep, group, span // row_count), f32),
             pltpu.VMEM((CHUNKS, n_ep, group, span // row_count), bf16),
             pltpu.VMEM((CHUNKS, n_ep, group, span // row_count), bf16),
@@ -326,48 +405,23 @@
         cost_estimate=pl.CostEstimate(
             flops=2 * all_rows * weight_count, bytes_accessed=2 * weight_count, transcendentals=0
         ),
-    )(message, stream, w_gate, w_up, w_down.reshape(experts * units, width))
-
-
-def local(
-    x_rows,
-    queries,
-    key_cache,
-    value_cache,
-    new_key,
-    new_value,
-    lengths,
-    norm_gain,
-    expert_ids,
-    gate_probs,
-    expert_place,
-    w_gate,
-    w_up,
-    w_down,
-):
-    row_count = x_rows.shape[0]
-    width = x_rows.shape[1]
-    stream = x_rows.astype(jnp.float32) + attend(
-        queries, key_cache, value_cache, new_key, new_value, lengths
+    )(
+        x_rows,
+        queries,
+        key_cache,
+        value_cache,
+        new_key,
+        new_value,
+        lengths,
+        norm_gain.reshape(1, width),
+        expert_ids,
+        gate_probs,
+        expert_place.reshape(1, -1),
+        w_gate,
+        w_up,
+        w_down.reshape(experts * units, width),
     )
-    scaled = lax.rsqrt(jnp.mean(stream * stream, axis=1, keepdims=True) + 1e-06)
-    normed = (stream * scaled * norm_gain.astype(jnp.float32)).astype(jnp.bfloat16)
-    experts_total = expert_place.shape[0]
-    expert_range = jnp.arange(experts_total, dtype=jnp.int32)
-    target = jnp.sum(jnp.where(expert_ids[:, :, None] == expert_range, expert_place, 0), axis=2)
-    table = jnp.sum(
-        jnp.where(target[:, :, None] == expert_range, gate_probs[:, :, None], 0.0), axis=1
-    )
-    high = lax.reduce_precision(table, 8, 7)
-    middle = lax.reduce_precision(table - high, 8, 7)
-    low = table - high - middle
-    pieces = jnp.stack([high, middle, low], axis=0).astype(jnp.bfloat16)
-    pieces = jnp.pad(pieces, ((0, row_count - 3), (0, 0), (0, 128 - experts_total)))
-    quarters = normed.reshape(row_count, row_count, width // row_count).transpose(1, 0, 2)
-    message = jnp.concatenate([quarters, pieces], axis=2).reshape(
-        row_count * row_count, width // row_count + 128
-    )
-    return run_experts(message, stream, w_gate, w_up, w_down)
+    return layer_out.astype(bf16), mixed.astype(bf16)
 
 
 def solution(mesh):

time: 50.7 us -> 43.1 us (0.85)
  local copies, waits for them, and re-layouts: 5.62 us -> 1.31 us
  matrix products: 1.57 us -> 0 us
  other arithmetic: 4.44 us -> 2.93 us
    unnamed x8 -> x0, local copies, waits for them, and re-layouts: 3.55 us -> none
    reduce_sum x4 -> x0, other arithmetic: 2.8 us -> none  [the longest x1 0.93 us: local(): scaled = lax.rsqrt(jnp.mean(stream * stream, axis=1, keepdims=True) + 1e-06)]
    convert_element_type x2, other arithmetic: 0.81 us -> 2.93 us  [local(): return (layer_out.astype(bf16), mixed.astype(bf16))]
    dot_general x3 -> x0, matrix products: 1.57 us -> none  [the longest x1 1.15 us: attend(): jnp.einsum('rgjd,rpgd->rgjp', query, cached_keys, precision=highest)]
    lt x1 -> x0, other arithmetic: 0.76 us -> none  [attend(): jnp.arange(span, dtype=jnp.int32)[None, :] < lengths[:, None]]
    mul x1 -> x0, local copies, waits for them, and re-layouts: 0.69 us -> none  [attend(): summed = summed + own_weight[..., None] * fresh_value[:, :, None, :]]
    reshape x3 -> x1, local copies, waits for them, and re-layouts: 1.36 us -> 1.31 us  [local(): norm_gain.reshape(1, width)]
where the time goes in v3:
time: 43.1 us; the launch traced here: 42.8 us
  Pallas kernels  37.9 us (88%)
  other arithmetic  2.93 us (7%)
  local copies, waits for them, and re-layouts  1.31 us (3%)
  between operations  0.64 us (1%)
    pallas_call x1, Pallas kernels, local(): pl.pallas_call(functools.partial(experts_kernel, n_ep, n_tp), out_shape=(...  37.9 us
    convert_element_type x2, other arithmetic, local(): return (layer_out.astype(bf16), mixed.astype(bf16))  2.93 us
    reshape x1, local copies, waits for them, and re-layouts, local(): norm_gain.reshape(1, width)  1.31 us

profile of v3, /device:TPU:0, one launch (start us, length us, event | category | flops | bytes accessed | tf_op | source)
XLA Modules:
  0.0 42.8 jit_solution(18104007654412195207)
XLA Ops:
  0.6 1.3 %reshape.13.gain_ref = bf16[1,4096]{1,0:T(2,128)(2,1)} reshape(bf16[4096]{0:T(1024)(128)(2,1)} %param.21) | data formatting | bytes 16384 | tf_op jit(solution)/shard_map/reshape | solution.py:416
  1.9 37.9 %shard_map.149 = (f32[4,4096]{1,0:T(4,128)}, f32[4,4096]{1,0:T(4,128)}) custom-call(bf16[4,4096]{1,0:T(4,128)(2,1)} %x_ref.1, bf16[4,4096]{1,0:T(4,128)(2,1)} %query_ref.1, bf16[4,64,256]{2,1,0:T(8,128)(2,1)} %key_ref.1, bf16[4,64,256]{2,1,0:T(8,128)(2,1)} %value_ref.1, bf16[4,256]{1,0:T(4,128)(2,1)} %new_key_ref.1, bf16[4,256]{1,0:T(4,128)(2,1)} %new_value_ref.1, ...), custom_call_target="tpu_custom_call" | custom-call | flops 2415919104 | bytes 37748736 | tf_op jit(solution)/shard_map/pallas_call | solution.py:371
  39.9 1.5 %convert_element_type.6 = bf16[4,4096]{1,0:T(4,128)(2,1)} convert(f32[4,4096]{1,0:T(4,128)} %get-tuple-element.4) | non-fusion elementwise | flops 16384 | bytes 98304 | tf_op jit(solution)/shard_map/convert_element_type | solution.py:424
  41.4 1.5 %convert_element_type.7 = bf16[4,4096]{1,0:T(4,128)(2,1)} convert(f32[4,4096]{1,0:T(4,128)} %get-tuple-element.5) | non-fusion elementwise | flops 16384 | bytes 98304 | tf_op jit(solution)/shard_map/convert_element_type | solution.py:424

commit v4 on v3

--- a/solution.py
+++ b/solution.py
@@ -70,7 +70,7 @@
     experts_total = place_ref.shape[1]
     rows = stream[...]
     scaled = lax.rsqrt(jnp.mean(rows * rows, axis=1, keepdims=True) + 1e-06)
-    normed = rows * scaled * gain_ref[...].astype(jnp.float32)
+    normed = rows * scaled * gain_ref[...].astype(jnp.float32).reshape(1, width)
     lane = lax.broadcasted_iota(jnp.int32, (row_count, 128), 1)
     ids, probs = ids_ref[...], prob_ref[...]
     table = jnp.zeros((row_count, 128), jnp.float32)
@@ -162,7 +162,6 @@
     down_load = pltpu.make_async_copy(w_down, down_v, weight_sem.at[2 * experts])
     for load in loads:
         load.start()
-    down_load.start()
 
     barrier = pltpu.get_barrier_semaphore()
     for j in range(1, n_ep):
@@ -213,6 +212,7 @@
                     copy.start()
                     across[m | b, s] = copy
                     sends.append(copy)
+    down_load.start()
 
     group = row_count * row_count
     to = lax.broadcasted_iota(jnp.int32, (block, n_ep * group), 0)
@@ -327,7 +327,7 @@
             place = slice(c * span + q * piece, c * span + (q + 1) * piece)
             mixed = packed_wide[c, 0, q * row_count : (q + 1) * row_count, :]
             mix_ref[:, place] = mixed
-            out_ref[:, place] = stream_ref[:, place] + mixed
+            out_ref[:, place] = stream_ref[:, place]
 
     stages = [compute] + [functools.partial(turn, k=k) for k in range(len(bits))] + [finish]
     for time in range(CHUNKS + len(stages) - 1):
@@ -368,7 +368,7 @@
     result = jax.ShapeDtypeStruct((row_count, width), f32)
     all_rows = n_tp * block
     weight_count = 3 * experts * width * units
-    layer_out, mixed = pl.pallas_call(
+    stream, mixed = pl.pallas_call(
         functools.partial(experts_kernel, n_ep, n_tp),
         out_shape=(result, result),
         in_specs=[vmem] * 6 + [smem] + [vmem] * 4 + [hbm] * 3,
@@ -413,7 +413,7 @@
         new_key,
         new_value,
         lengths,
-        norm_gain.reshape(1, width),
+        norm_gain,
         expert_ids,
         gate_probs,
         expert_place.reshape(1, -1),
@@ -421,7 +421,7 @@
         w_up,
         w_down.reshape(experts * units, width),
     )
-    return layer_out.astype(bf16), mixed.astype(bf16)
+    return (stream + mixed).astype(bf16), mixed.astype(bf16)
 
 
 def solution(mesh):

time: 43.1 us -> 40.4 us (0.937)
  other arithmetic: 2.93 us -> 1.57 us
  local copies, waits for them, and re-layouts: 1.31 us -> 0 us
    convert_element_type x2 -> x1, other arithmetic: 2.93 us -> 1.57 us  [local(): return ((stream + mixed).astype(bf16), mixed.astype(bf16))]
    reshape x1 -> x0, local copies, waits for them, and re-layouts: 1.31 us -> none  [local(): norm_gain.reshape(1, width)]
where the time goes in v4:
time: 40.4 us; the launch traced here: 40.2 us
  Pallas kernels  38 us (94%)
  other arithmetic  1.57 us (4%)
  between operations  0.64 us (2%)
    pallas_call x1, Pallas kernels, local(): pl.pallas_call(functools.partial(experts_kernel, n_ep, n_tp), out_shape=(...  38 us
    convert_element_type x1, other arithmetic, local(): return ((stream + mixed).astype(bf16), mixed.astype(bf16))  1.57 us

profile of v4, /device:TPU:0, one launch (start us, length us, event | category | flops | bytes accessed | tf_op | source)
XLA Modules:
  0.0 40.2 jit_solution(8591229013600665835)
XLA Ops:
  0.6 38.0 %shard_map.149 = (f32[4,4096]{1,0:T(4,128)}, f32[4,4096]{1,0:T(4,128)}) custom-call(bf16[4,4096]{1,0:T(4,128)(2,1)} %x_ref.1, bf16[4,4096]{1,0:T(4,128)(2,1)} %query_ref.1, bf16[4,64,256]{2,1,0:T(8,128)(2,1)} %key_ref.1, bf16[4,64,256]{2,1,0:T(8,128)(2,1)} %value_ref.1, bf16[4,256]{1,0:T(4,128)(2,1)} %new_key_ref.1, bf16[4,256]{1,0:T(4,128)(2,1)} %new_value_ref.1, ...), custom_call_target="tpu_custom_call" | custom-call | flops 2415919104 | bytes 37748736 | tf_op jit(solution)/shard_map/pallas_call | solution.py:371
  38.6 1.6 %fusion = (bf16[4,4096]{1,0:T(4,128)(2,1)}, bf16[4,4096]{1,0:T(4,128)(2,1)}) fusion(f32[4,4096]{1,0:T(4,128)} %get-tuple-element.5, f32[4,4096]{1,0:T(4,128)} %get-tuple-element.4), kind=kLoop, calls=%fused_computation.1 | loop fusion | flops 49152 | bytes 196608 | tf_op jit(solution)/shard_map/convert_element_type | solution.py:424
